TPU v7x, 512 devices: a whole 4x4x16 slice. The times are simulated.
512 devices in a mesh: row: 16 (over z_lo, x), col: 8 (over y, core), day: 4 (over z_hi).
Axes of the slice: x: 4, y: 4, z: 16 (z_hi: 4, z_lo: 4; z = z_hi * 4 + z_lo), core: 2. Of those that a mesh axis runs over, the one named last changes fastest.
Arguments:
- noise: bfloat16 [4, 8, 4096, 1500], P('day', 'col', 'row'), may hold values from -25 to 25
- keep: int32 [4, 8, 4096], P('day', 'col', 'row'), may hold values 0 or 1
Outputs:
- stacked: float32 [128, 51, 4096], P(('col', 'day'), None, 'row')
All inputs are finite; a program needn't handle non-finite values. No bound on the sum of `keep` on one device may be relied on, other than what follows from the above.
Results may differ from a plain program's by a relative error of at most 0.02.
Values may be sent and summed in bfloat16 or wider, within the bound.
A program may use at most 64 MiB of HBM per device.

v0:
```python
import math

import jax
import jax.numpy as jnp
from jax import lax
from jax.sharding import PartitionSpec as P

F = 256
LOW = 60
HALF = 64
MAXLAG = 25
SRC_DEV = 16


def split_product(left, right_table):
    table_high = right_table.astype(jnp.bfloat16)
    table_rest = (right_table - table_high.astype(jnp.float32)).astype(jnp.bfloat16)
    return jnp.dot(left, table_high, preferred_element_type=jnp.float32) + jnp.dot(
        left, table_rest, preferred_element_type=jnp.float32
    )


def shards(noise, keep):
    win_local = noise.shape[1]
    channels = noise.shape[2]
    sample_total = noise.shape[3]
    row_count = lax.axis_size("row")
    col_count = lax.axis_size("col")
    day_count = lax.axis_size("day")
    time_index = jnp.arange(sample_total, dtype=jnp.int32)
    bin_index = jnp.arange(F, dtype=jnp.int32)
    phases = jnp.mod((LOW + bin_index)[None, :] * time_index[:, None], sample_total)
    angles = 2.0 * math.pi / sample_total * phases.astype(jnp.float32)
    twiddle = jnp.concatenate([jnp.cos(angles), -jnp.sin(angles)], axis=1)
    samples = noise[0].reshape(win_local * channels, sample_total)
    product = split_product(samples, twiddle)
    real_part = product[:, :F]
    imag_part = product[:, F:]
    magnitude = jnp.sqrt(real_part * real_part + imag_part * imag_part)
    band_float = (jnp.abs(bin_index[:, None] - bin_index[None, :]) <= HALF).astype(jnp.float32)
    band_matrix = band_float.astype(jnp.bfloat16)
    magnitude_high = magnitude.astype(jnp.bfloat16)
    magnitude_rest = (magnitude - magnitude_high.astype(jnp.float32)).astype(jnp.bfloat16)
    band_total = jnp.dot(magnitude_high, band_matrix, preferred_element_type=jnp.float32) + jnp.dot(
        magnitude_rest, band_matrix, preferred_element_type=jnp.float32
    )
    levels = band_total / jnp.sum(band_float, axis=0) + 1e-06
    keep_float = keep[0].astype(jnp.float32).reshape(win_local * channels, 1)
    whitened = jnp.stack(
        [
            (keep_float * real_part / levels).astype(jnp.bfloat16),
            (keep_float * imag_part / levels).astype(jnp.bfloat16),
        ]
    ).reshape(2, win_local, channels, F)
    keep_flags = keep[0].astype(jnp.bfloat16)
    whitened_all, flags_all = (
        lax.all_gather(whitened, "col", axis=1, tiled=True),
        lax.all_gather(keep_flags, "col", axis=0, tiled=True),
    )
    win_total = whitened_all.shape[1]
    stride = channels * row_count // (SRC_DEV * col_count)
    local_sources = whitened_all[:, :, ::stride, :]
    local_flags = flags_all[:, ::stride]
    col_index = lax.axis_index("col")
    wanted = col_index * SRC_DEV + jnp.arange(SRC_DEV, dtype=jnp.int32)
    initial = (
        jnp.zeros((2, win_total, SRC_DEV, F), jnp.bfloat16),
        jnp.zeros((1, win_total, SRC_DEV), jnp.bfloat16),
    )
    shard_piece = (
        lax.all_gather(local_sources, "row", axis=2, tiled=True),
        lax.all_gather(local_flags[None], "row", axis=2, tiled=True),
    )
    piece_count = shard_piece[0].shape[2]
    inside = (wanted >= 0) & (wanted < piece_count)
    positions = jnp.clip(wanted, 0, piece_count - 1)
    spectra_pick = jnp.take(shard_piece[0], positions, axis=2)
    flags_pick = jnp.take(shard_piece[1], positions, axis=2)
    sources = jnp.where(inside[None, None, :, None], spectra_pick, initial[0])
    picked_flags = jnp.where(inside[None, None, :], flags_pick, initial[1])
    source_flags = picked_flags[0]
    pair_counts = jnp.einsum(
        "ws,wc->sc", source_flags, flags_all, preferred_element_type=jnp.float32
    )
    pair_floor = jnp.maximum(pair_counts, 1.0)
    lag_total = 2 * MAXLAG + 1
    lag_index = jnp.arange(lag_total, dtype=jnp.int32) - MAXLAG
    lag_phase = jnp.mod((LOW + bin_index)[None, :] * lag_index[:, None], sample_total)
    lag_angle = 2.0 * math.pi / sample_total * lag_phase.astype(jnp.float32)
    cosine = jnp.cos(lag_angle).astype(jnp.bfloat16)
    sine = jnp.sin(lag_angle).astype(jnp.bfloat16)
    norm_factor = 1.0 / math.sqrt(F)
    bin_block = min(32, F)
    stacked = jnp.zeros(
        (SRC_DEV // day_count * lax.axis_size("day"), lag_total, channels), jnp.float32
    )
    for block_start in range(0, F, bin_block):
        block_end = block_start + bin_block
        chan_real = whitened_all[0, :, :, block_start:block_end]
        chan_imag = whitened_all[1, :, :, block_start:block_end]
        src_real = sources[0, :, :, block_start:block_end]
        src_imag = sources[1, :, :, block_start:block_end]
        cross_real = jnp.einsum(
            "wsf,wcf->fsc", src_real, chan_real, preferred_element_type=jnp.float32
        ) + jnp.einsum("wsf,wcf->fsc", src_imag, chan_imag, preferred_element_type=jnp.float32)
        cross_imag = jnp.einsum(
            "wsf,wcf->fsc", src_real, chan_imag, preferred_element_type=jnp.float32
        ) - jnp.einsum("wsf,wcf->fsc", src_imag, chan_real, preferred_element_type=jnp.float32)
        normed_real = (cross_real / pair_floor[None]).astype(jnp.bfloat16)
        normed_imag = (cross_imag / pair_floor[None]).astype(jnp.bfloat16)
        stacked = (
            stacked
            + jnp.einsum(
                "lf,fsc->slc",
                cosine[:, block_start:block_end],
                normed_real,
                preferred_element_type=jnp.float32,
            )
            - jnp.einsum(
                "lf,fsc->slc",
                sine[:, block_start:block_end],
                normed_imag,
                preferred_element_type=jnp.float32,
            )
        )
    return lax.psum_scatter(
        (stacked * norm_factor).astype(jnp.bfloat16), "day", scatter_dimension=0, tiled=True
    ).astype(jnp.float32)


def solution(mesh):
    in_specs = (P("day", "col", "row", None), P("day", "col", "row"))
    out_specs = P(("col", "day"), None, "row")
    return jax.shard_map(shards, mesh=mesh, in_specs=in_specs, out_specs=out_specs, check_vma=False)
```

profile of v0, /device:TPU:1, one launch (start us, length us, event | category | flops | bytes accessed | tf_op | source)
XLA Modules:
  0.0 285.0 jit_solution(15595979797675692308)
XLA Ops:
  6.6 6.3 %fusion.7 = (f32[1500,256]{1,0:T(8,128)S(1)}, f32[1500,256]{1,0:T(8,128)S(1)}) fusion(s32[256]{0:T(256)S(1)} %iota_add_fusion), kind=kLoop, calls=%fused_computation.13 | loop fusion | flops 3840000 | bytes 3073024 | tf_op jit(solution)/shard_map/cos | solution.py:34
  12.9 0.6 fusion.1
  13.5 0.6 fusion.30
  14.5 0.3 fusion.75
  14.8 0.7 pad_maximum_fusion.1
  15.7 40.8 %all-gather.8.cloned.1.call-done = bf16[2,2048,256]{1,2,0:T(8,128)(2,1)} async-done(((bf16[2,256,256]{1,2,0:T(8,128)(2,1)}), bf16[2,2048,256]{1,2,0:T(8,128)(2,1)}) %all-gather.8.cloned.1.call-update) | async-done | bytes 2097168 | tf_op jit(solution)/shard_map/all_gather | solution.py:57
  56.4 2.3 copy.148
  58.7 10.0 %slice.158 = bf16[2,8,8,256]{2,1,3,0:T(8,128)(2,1)} slice(bf16[2,8,256,256]{2,1,3,0:T(8,128)(2,1)S(1)} %bitcast.205), slice={[0:2:1], [0:8:1], [0:256:32], [0:256:1]} | slice | bytes 131072 | tf_op jit(solution)/shard_map/slice | solution.py:62
  68.8 2.5 copy.94
  71.4 9.9 %all-gather.1 = bf16[8,1,256]{2,1,0:T(2,128)(2,1)S(1)} all-gather(bf16[1,1,256]{2,1,0:T(2,128)(2,1)S(1)} %get-tuple-element.25), channel_id=3, replica_groups=mesh['row'=16,'col'=8,'day'=4] {'col'}, dimensions={0}, use_global_device_ids=true | all-gather | bytes 4608 | tf_op jit(solution)/shard_map/all_gather | solution.py:58
  81.5 36.0 %all-gather.2 = bf16[8,128]{0,1:T(8,128)(2,1)S(1)} all-gather(bf16[8,8]{0,1:T(8,128)(2,1)S(1)} %slice.163), channel_id=4, replica_groups=mesh['row'=16,'col'=8,'day'=4] {'row'}, dimensions={1}, use_global_device_ids=true | all-gather | bytes 2176 | tf_op jit(solution)/shard_map/all_gather | solution.py:72
  117.5 0.6 gather_fusion.1
  118.1 0.8 convolution_maximum_fusion
  118.9 1.2 sine_convert_fusion
  120.1 28.3 %all-gather.6.cloned.1.call-done = bf16[2,8,128,256]{3,1,0,2:T(8,128)(2,1)} async-done(((bf16[2,8,8,256]{3,1,0,2:T(8,128)(2,1)}), bf16[2,8,128,256]{3,1,0,2:T(8,128)(2,1)}) %all-gather.6.cloned.1.call-update) | async-done | bytes 1048592 | tf_op jit(solution)/shard_map/all_gather | solution.py:71
  148.4 2.3 copy.95
  150.7 1.8 gather_fusion
  152.6 0.9 slice_bitcast_fusion.48
  153.6 2.0 fusion.78
  155.6 2.0 fusion.79
  157.7 2.0 fusion.80
  159.7 2.0 fusion.81
  161.8 2.0 fusion.82
  163.7 2.0 fusion.83
  165.9 2.0 fusion.84
  167.8 2.0 fusion.85
  169.9 2.0 fusion.86
  171.9 2.0 fusion.87
  174.0 2.0 fusion.88
  176.0 1.2 fusion.89
  177.3 1.2 fusion.90
  178.5 1.2 fusion.91
  179.8 1.2 fusion.92
  181.0 1.2 fusion.93
  182.2 1.5 copy.97
  183.7 2.2 fusion.46
  185.8 2.1 fusion.45
  188.0 0.7 copy.104
  188.7 2.2 fusion.44
  190.9 2.2 fusion.43
  193.0 0.7 copy.110
  193.8 2.1 fusion.42
  195.9 2.1 fusion.41
  198.1 0.7 copy.116
  198.8 2.2 fusion.40
  201.0 2.1 fusion.39
  203.1 0.7 copy.122
  203.8 2.1 fusion.38
  206.0 2.1 fusion.37
  208.1 0.7 copy.128
  208.8 2.1 fusion.36
  211.0 1.9 fusion.35
  213.0 1.2 fusion.34
  214.2 1.2 fusion.33
  215.5 1.2 fusion.32
  216.8 1.2 fusion.31
  218.9 0.3 convolution_add_fusion.6
  219.3 0.3 convolution_subtract_fusion.6
  220.3 0.3 convolution_subtract_fusion.5
  221.2 0.3 convolution_subtract_fusion.4
  223.5 0.3 convolution_add_fusion.1
  224.5 1.1 fusion.12
  225.6 51.2 %reduce-scatter.2.cloned.1.call-done = bf16[4,51,256]{2,1,0:T(8,128)(2,1)} async-done(((bf16[16,51,256]{2,1,0:T(8,128)(2,1)}), bf16[4,51,256]{2,1,0:T(8,128)(2,1)}) %reduce-scatter.2.cloned.1.call-update) | async-done | bytes 104464 | tf_op jit(solution)/shard_map/reduce_scatter | solution.py:126
  276.8 1.6 copy.145
  (85 shorter events, 6.8 us)
Async XLA Ops:
  6.5 6.3 %copy-start = (bf16[1,1,256,1500]{2,3,1,0:T(8,128)(2,1)S(1)}, bf16[1,1,256,1500]{2,3,1,0:T(8,128)(2,1)}, u32[]{:S(2)}) copy-start(bf16[1,1,256,1500]{2,3,1,0:T(8,128)(2,1)} %param.2) | copy-start | bytes 2304004
  6.5 49.9 %all-gather.8.cloned.1.call-start = ((), (), s32[]{:S(2)}) async-start(), calls=%async_computation.3 | async-start | bytes 2359296 | tf_op jit(solution)/shard_map/all_gather | solution.py:57
  13.5 0.7 copy-start.21
  15.6 132.8 %all-gather.6.cloned.1.call-start = ((), (), s32[]{:S(2)}) async-start(), calls=%async_computation.1 | async-start | bytes 1114112 | tf_op jit(solution)/shard_map/all_gather | solution.py:71
  58.7 92.0 %copy-start.1 = (bf16[64,8,8,256]{3,2,1,0:T(8,128)(2,1)}, bf16[64,8,8,256]{3,2,1,0:T(8,128)(2,1)S(1)}, u32[]{:S(2)}) copy-start(bf16[64,8,8,256]{3,2,1,0:T(8,128)(2,1)S(1)} %copy.148) | copy-start | bytes 6291460
  71.3 205.5 %reduce-scatter.2.cloned.1.call-start = ((), (), s32[]{:S(2)}) async-start(), calls=%async_computation.2 | async-start | bytes 573440 | tf_op jit(solution)/shard_map/reduce_scatter | solution.py:126
  182.2 5.8 %copy-start.20 = (bf16[8,16,32]{2,0,1:T(8,128)(2,1)S(1)}, bf16[8,16,32]{2,0,1:T(8,128)(2,1)}, u32[]{:S(2)}) copy-start(bf16[8,16,32]{2,0,1:T(8,128)(2,1)} %get-tuple-element.19) | copy-start | bytes 24580
  188.0 5.1 %copy-start.19 = (bf16[8,16,32]{2,0,1:T(8,128)(2,1)S(1)}, bf16[8,16,32]{2,0,1:T(8,128)(2,1)}, u32[]{:S(2)}) copy-start(bf16[8,16,32]{2,0,1:T(8,128)(2,1)} %get-tuple-element.17) | copy-start | bytes 24580
  193.0 5.0 %copy-start.18 = (bf16[8,16,32]{2,0,1:T(8,128)(2,1)S(1)}, bf16[8,16,32]{2,0,1:T(8,128)(2,1)}, u32[]{:S(2)}) copy-start(bf16[8,16,32]{2,0,1:T(8,128)(2,1)} %get-tuple-element.15) | copy-start | bytes 24580
  198.1 5.0 %copy-start.17 = (bf16[8,16,32]{2,0,1:T(8,128)(2,1)S(1)}, bf16[8,16,32]{2,0,1:T(8,128)(2,1)}, u32[]{:S(2)}) copy-start(bf16[8,16,32]{2,0,1:T(8,128)(2,1)} %get-tuple-element.13) | copy-start | bytes 24580
  203.1 5.0 %copy-start.16 = (bf16[8,16,32]{2,0,1:T(8,128)(2,1)S(1)}, bf16[8,16,32]{2,0,1:T(8,128)(2,1)}, u32[]{:S(2)}) copy-start(bf16[8,16,32]{2,0,1:T(8,128)(2,1)} %get-tuple-element.11) | copy-start | bytes 24580
  208.1 4.8 %copy-start.15 = (bf16[8,16,32]{2,0,1:T(8,128)(2,1)S(1)}, bf16[8,16,32]{2,0,1:T(8,128)(2,1)}, u32[]{:S(2)}) copy-start(bf16[8,16,32]{2,0,1:T(8,128)(2,1)} %get-tuple-element.9) | copy-start | bytes 24580
  208.8 4.2 %copy-start.22 = (f32[16,256]{1,0:T(8,128)S(1)}, f32[16,256]{1,0:T(8,128)}, u32[]{:S(2)}) copy-start(f32[16,256]{1,0:T(8,128)} %convolution_maximum_fusion) | copy-start | bytes 49156
  212.9 2.7 copy-start.23
  215.4 2.6 copy-start.2
  215.4 2.6 copy-start.3
  215.5 2.8 copy-start.4
  218.0 1.0 copy-start.6
  218.3 1.0 copy-start.5
  218.9 1.0 copy-start.8
  219.3 1.0 copy-start.7
  219.9 1.0 copy-start.10
  220.3 1.0 copy-start.9
  220.9 1.0 copy-start.12
  221.2 1.0 copy-start.11
  221.8 1.0 copy-start.14
  222.2 1.0 copy-start.13
Sparse Core Ops, SparseCore 0:
  15.7 40.6 all-gather.7
  71.5 76.9 all-gather.5
  225.8 51.0 reduce-scatter.1
where the time goes:
time: 286 us; the launch traced here: 285 us
  waiting for transfers between devices  120 us (42%)
  matrix products  66.5 us (23%)
  blocking collectives  45.9 us (16%)
  local copies, waits for them, and re-layouts  30.2 us (11%)
  between operations  13.5 us (5%)
  other arithmetic  8.44 us (3%)
    reduce_scatter x1, waiting for transfers between devices, shards(): lax.psum_scatter((stacked * norm_factor).astype(jnp.bfloat16), 'day', sca...  51.2 us
    all_gather x1, waiting for transfers between devices, shards(): lax.all_gather(whitened, 'col', axis=1, tiled=True)  40.8 us
    all_gather x1, blocking collectives, shards(): lax.all_gather(local_flags[None], 'row', axis=2, tiled=True)  36 us
    all_gather x1, waiting for transfers between devices, shards(): lax.all_gather(local_sources, 'row', axis=2, tiled=True)  28.3 us
    dot_general x8, matrix products, shards(): jnp.einsum('wsf,wcf->fsc', src_imag, chan_imag, preferred_element_type=jn...  15.3 us
    dot_general x8, matrix products, shards(): jnp.einsum('wsf,wcf->fsc', src_imag, chan_real, preferred_element_type=jn...  14.9 us
    dot_general x8, matrix products, shards(): jnp.einsum('wsf,wcf->fsc', src_real, chan_real, preferred_element_type=jn...  14.3 us
    dot_general x8, matrix products, shards(): jnp.einsum('wsf,wcf->fsc', src_real, chan_imag, preferred_element_type=jn...  13.4 us
  transfers between devices with their start and end apart: 3, of which 3 were waited for; matrix products, arithmetic and copies ran while one was open for 1% of the time, Pallas kernels for 0%

commit v1 on v0

v1 whole, which is shorter than its diff:
```python
import functools
import math

import jax
import jax.numpy as jnp
import ml_dtypes
import numpy as np
from jax import lax
from jax.experimental import pallas as pl
from jax.experimental.pallas import tpu as pltpu
from jax.sharding import PartitionSpec as P

MESH = pl.DeviceIdType.MESH
BF16 = jnp.bfloat16
F32 = jnp.float32

F = 256
LOW = 60
HALF = 64
MAXLAG = 25
LAGS = 2 * MAXLAG + 1
TLEN = 1500
CH = 256
WIN = 8
GROUP = 4
ROWS = 208
TOP = 112
KROWS = 2 * F + 16
FIRST = 272
SLANES = F + 128
H = 1
CP = CH // H


def tables():
    k = np.arange(F)
    t = np.arange(TLEN)
    angle = 2.0 * np.pi / TLEN * ((LOW + k)[:, None] * t[None, :] % TLEN)
    twiddle = np.concatenate([np.cos(angle), -np.sin(angle)], axis=0).astype(np.float32)
    high = twiddle.astype(ml_dtypes.bfloat16)
    rest = (twiddle - high.astype(np.float32)).astype(ml_dtypes.bfloat16)
    band = (np.abs(k[:, None] - k[None, :]) <= HALF).astype(ml_dtypes.bfloat16)
    lag = np.arange(LAGS) - MAXLAG
    lag_angle = 2.0 * np.pi / TLEN * ((LOW + k)[None, :] * lag[:, None] % TLEN)
    cosine = np.zeros((ROWS, F), np.float32)
    sine = np.zeros((ROWS, F), np.float32)
    cosine[: GROUP * LAGS] = np.repeat(np.cos(lag_angle), GROUP, axis=0)
    sine[: GROUP * LAGS] = np.repeat(np.sin(lag_angle), GROUP, axis=0)
    rep = np.zeros((64, 16), ml_dtypes.bfloat16)
    for g in range(2):
        for part in range(2):
            for i in range(16):
                rep[g * 32 + part * 16 + i, part * 8 + g * GROUP + i % GROUP] = 1
    pick = np.zeros((16, CH), ml_dtypes.bfloat16)
    for i in range(16):
        pick[i, (i % 8) * 32] = 1
    return (
        high,
        rest,
        band,
        cosine.astype(ml_dtypes.bfloat16),
        sine.astype(ml_dtypes.bfloat16),
        rep,
        pick,
    )


def kernel(
    noise, keep, high, rest, band, cosine, sine, rep, pick, out,
    wall, sown, sfin, tmat, flags, acc, part, fold_up, fold_down, got_up, got_down,
    w_send, w_recv, s1_send, s1_recv, s2_send, s2_recv, s3_send, s3_recv, d_send, d_recv,
):
    row, col, day = lax.axis_index("row"), lax.axis_index("col"), lax.axis_index("day")
    z, x = row // 4, row % 4
    y, core = col // 2, col % 2
    side = x % 2
    holder = core == x // 2
    collector = jnp.logical_and(holder, y == z)
    upper = ((y + 1) % 4) * 2 + core
    lower = ((y + 3) % 4) * 2 + core
    far = ((y + 2) % 4) * 2 + core
    sibling = y * 2 + 1 - core

    def device(r=row, c=col, d=day):
        return (r, c, d)

    def remote(src, dst, send, recv, target):
        return pltpu.make_async_remote_copy(
            src_ref=src, dst_ref=dst, send_sem=send, recv_sem=recv,
            device_id=target, device_id_type=MESH,
        )

    barrier = pltpu.get_barrier_semaphore()
    partners = [device(c=(col + i) % 8) for i in range(1, 8)]
    partners += [device(r=z * 4 + (x + i) % 4) for i in range(1, 4)]
    partners += [device(r=((z + i) % 4) * 4 + x) for i in range(1, 4)]
    partners += [device(d=(day + i) % 4) for i in (1, 3)]
    for partner in partners:
        pl.semaphore_signal(barrier, inc=1, device_id=partner, device_id_type=MESH)

    spectrum = jnp.dot(high[...], noise[...], preferred_element_type=F32)
    spectrum += jnp.dot(rest[...], noise[...], preferred_element_type=F32)
    real, imag = spectrum[:F], spectrum[F:]
    magnitude = jnp.sqrt(real * real + imag * imag)
    total = jnp.dot(band[...], magnitude.astype(BF16), preferred_element_type=F32)
    bins = lax.broadcasted_iota(jnp.int32, (F, CH), 0)
    count = jnp.minimum(bins + HALF, F - 1) - jnp.maximum(bins - HALF, 0) + 1
    levels = total / count.astype(F32) + 1e-6
    keep_row = keep[...].astype(F32)
    scale = keep_row / levels
    white = jnp.concatenate([real * scale, imag * scale], axis=0).astype(BF16)
    keep_rows = jnp.broadcast_to(keep_row, (16, CH)).astype(BF16)
    for h in range(H):
        cut = slice(h * CP, (h + 1) * CP)
        wall[h, col, 0 : 2 * F, :] = white[:, cut]
        wall[h, col, 2 * F : KROWS, :] = keep_rows[:, cut]

    picked = lax.dot_general(
        pick[...], white, (((1,), (1,)), ((), ())), preferred_element_type=F32
    )
    lower_half = lax.broadcasted_iota(jnp.int32, (16, F), 0) < 8
    mixed = jnp.where(lower_half, picked[:, :F], picked[:, F:])
    flag = jnp.sum(pick[...].astype(F32) * keep_row, axis=1, keepdims=True)
    message = jnp.concatenate([mixed, jnp.broadcast_to(flag, (16, 128))], axis=1).astype(BF16)

    pl.semaphore_wait(barrier, len(partners))

    @pl.when(collector)
    def _():
        sfin[side, col] = message

    @pl.when(jnp.logical_not(collector))
    def _():
        sown[...] = message
        remote(
            sown, sfin.at[side, col], s1_send, s1_recv.at[col], device(c=row // 2)
        ).start()

    def block(h, w, rows=None):
        if rows is None:
            return wall.at[h, w]
        return wall.at[h, w, pl.ds(rows[0], rows[1]), :]

    top, bottom = (0, FIRST), (FIRST, KROWS - FIRST)

    def w_copy(h, index):
        w, rows, target = [
            (col, None, upper),
            (col, None, lower),
            (col, None, sibling),
            (lower, None, sibling),
            (upper, None, sibling),
            (lower, top, upper),
            (upper, bottom, lower),
            (far, top, sibling),
            (far, bottom, sibling),
        ][index]
        ref = block(h, w, rows)
        return remote(ref, ref, w_send.at[h, index], w_recv.at[h, index], device(c=target))

    other = 1 - core

    def w_arrival(h, index):
        w, rows = [
            (lower, None),
            (upper, None),
            (sibling, None),
            (((y + 3) % 4) * 2 + other, None),
            (((y + 1) % 4) * 2 + other, None),
            (far, top),
            (far, bottom),
            (((y + 2) % 4) * 2 + other, top),
            (((y + 2) % 4) * 2 + other, bottom),
        ][index]
        ref = block(h, w, rows)
        remote(ref, ref, w_send.at[h, index], w_recv.at[h, index], device(c=sibling)).wait_recv()

    for h in range(H):
        for index in (0, 1, 2):
            w_copy(h, index).start()

    def s2_copy(i):
        ref = sfin.at[side]
        return remote(ref, ref, s2_send.at[i - 1], s2_recv, device(r=((z + i) % 4) * 4 + x))

    def s3_copy(i):
        ref = sfin.at[side]
        return remote(
            ref, ref, s3_send.at[i - 1], s3_recv.at[side], device(r=z * 4 + (x + i) % 4)
        )

    @pl.when(collector)
    def _():
        for i in range(1, 8):
            w = (col + i) % 8
            remote(
                sown, sfin.at[side, w], s1_send, s1_recv.at[w], device(c=(col + i) % 8)
            ).wait_recv()
        for i in (1, 2, 3):
            s2_copy(i).start()

    @pl.when(jnp.logical_and(holder, jnp.logical_not(collector)))
    def _():
        s2_copy(1).wait_recv()

    @pl.when(holder)
    def _():
        for i in (1, 2, 3):
            s3_copy(i).start()

    for h in range(H):
        w_arrival(h, 0)
        w_copy(h, 3).start()
        w_copy(h, 5).start()
        w_arrival(h, 1)
        w_copy(h, 4).start()
        w_copy(h, 6).start()

    for e in range(2):
        @pl.when(jnp.logical_not(jnp.logical_and(holder, side == e)))
        def _():
            ref = sfin.at[e]
            remote(ref, ref, s3_send.at[0], s3_recv.at[e], device(r=z * 4 + (x + 1) % 4)).wait_recv()

        def make(w, carry):
            spread = jnp.dot(rep[...], sfin[e, w], preferred_element_type=F32)
            for g in range(2):
                base = 32 * g
                s_real = spread[base : base + 16, :F].astype(BF16)[None]
                s_imag = spread[base + 16 : base + 32, :F].astype(BF16)[None]
                flags[w, 2 * e + g] = spread[base : base + 16, F:]
                cos3 = cosine[...].reshape(ROWS // 16, 16, F)
                sin3 = sine[...].reshape(ROWS // 16, 16, F)
                t_real = s_real * cos3 + s_imag * sin3
                t_imag = s_imag * cos3 - s_real * sin3
                tmat[w, 2 * e + g, :, :F] = t_real.reshape(ROWS, F)
                tmat[w, 2 * e + g, :, F:] = t_imag.reshape(ROWS, F)
            return carry

        lax.fori_loop(0, WIN, make, 0)

    for h in range(H):
        def add(w, first=False):
            def body(d, carry):
                value = jnp.dot(
                    tmat[w, d], wall[h, w, 0 : 2 * F, :], preferred_element_type=F32
                )
                acc[d] = value if first else acc[d] + value
                return carry
            lax.fori_loop(0, 4, body, 0)

        add(col, True)
        w_arrival(h, 2)
        add(sibling)
        add(lower)
        add(upper)
        w_arrival(h, 3)
        add(((y + 3) % 4) * 2 + other)
        w_arrival(h, 4)
        add(((y + 1) % 4) * 2 + other)
        w_arrival(h, 5)
        w_copy(h, 7).start()
        w_arrival(h, 6)
        w_copy(h, 8).start()
        add(far)
        w_arrival(h, 7)
        w_arrival(h, 8)
        add(((y + 2) % 4) * 2 + other)

        def partial(d):
            pairs = jnp.zeros((16, CP), F32)
            for w in range(WIN):
                kept = wall[h, w, 2 * F : KROWS, :].astype(F32)
                flag = flags[w, d]
                if CP == CH:
                    flag = jnp.concatenate([flag, flag], axis=1)
                pairs += flag * kept
            inverse = (1.0 / math.sqrt(F)) / jnp.maximum(pairs, 1.0)
            return (acc[d].reshape(ROWS // 16, 16, CP) * inverse[None]).reshape(ROWS, CP)

        def d_copy(index):
            src, dst, target = [
                (part.at[h, 0, pl.ds(0, TOP), :], fold_up.at[h], 1),
                (part.at[h, 0, pl.ds(TOP, ROWS - TOP), :], fold_down.at[h], 3),
                (part.at[h, 1], got_up.at[h], 1),
                (part.at[h, 2], got_down.at[h], 3),
            ][index]
            return remote(
                src, dst, d_send.at[h, index], d_recv.at[h, index], device(d=(day + target) % 4)
            )

        part[h, 0] = partial((day + 2) % 4).astype(BF16)
        d_copy(0).start()
        d_copy(1).start()
        plus = partial((day + 1) % 4)
        minus = partial((day + 3) % 4)
        own = partial(day)
        d_copy(0).wait_recv()
        part[h, 1, 0:TOP, :] = (plus[:TOP] + fold_up[h].astype(F32)).astype(BF16)
        part[h, 1, TOP:, :] = plus[TOP:].astype(BF16)
        d_copy(2).start()
        d_copy(1).wait_recv()
        part[h, 2, 0:TOP, :] = minus[:TOP].astype(BF16)
        part[h, 2, TOP:, :] = (minus[TOP:] + fold_down[h].astype(F32)).astype(BF16)
        d_copy(3).start()
        d_copy(2).wait_recv()
        d_copy(3).wait_recv()
        result = own + got_up[h].astype(F32) + got_down[h].astype(F32)
        out[:, h * CP : (h + 1) * CP] = result

    @pl.when(jnp.logical_not(collector))
    def _():
        remote(
            sown, sfin.at[side, col], s1_send, s1_recv.at[col], device(c=row // 2)
        ).wait_send()

    @pl.when(collector)
    def _():
        for i in (1, 2, 3):
            s2_copy(i).wait_send()

    @pl.when(holder)
    def _():
        for i in (1, 2, 3):
            s3_copy(i).wait_send()

    for h in range(H):
        for index in range(9):
            w_copy(h, index).wait_send()
        for index in range(4):
            d_copy(index).wait_send()


def shards(noise, keep):
    samples = noise[0, 0].T
    consts = tables()
    dma = pltpu.SemaphoreType.DMA
    result = pl.pallas_call(
        kernel,
        out_shape=jax.ShapeDtypeStruct((ROWS, CH), F32),
        in_specs=[pl.BlockSpec(memory_space=pltpu.VMEM)] * (2 + len(consts)),
        out_specs=pl.BlockSpec(memory_space=pltpu.VMEM),
        scratch_shapes=[
            pltpu.VMEM((H, WIN, KROWS, CP), BF16),
            pltpu.VMEM((16, SLANES), BF16),
            pltpu.VMEM((2, WIN, 16, SLANES), BF16),
            pltpu.VMEM((WIN, 4, ROWS, 2 * F), BF16),
            pltpu.VMEM((WIN, 4, 16, 128), F32),
            pltpu.VMEM((4, ROWS, CP), F32),
            pltpu.VMEM((H, 3, ROWS, CP), BF16),
            pltpu.VMEM((H, TOP, CP), BF16),
            pltpu.VMEM((H, ROWS - TOP, CP), BF16),
            pltpu.VMEM((H, ROWS, CP), BF16),
            pltpu.VMEM((H, ROWS, CP), BF16),
            dma((H, 9)),
            dma((H, 9)),
            dma,
            dma((8,)),
            dma((3,)),
            dma,
            dma((3,)),
            dma((2,)),
            dma((H, 4)),
            dma((H, 4)),
        ],
        compiler_params=pltpu.CompilerParams(
            collective_id=0, has_side_effects=True, vmem_limit_bytes=48 * 1024 * 1024
        ),
    )(samples, keep[0], *[jnp.asarray(c) for c in consts])
    return result[: GROUP * LAGS].reshape(LAGS, GROUP, CH).transpose(1, 0, 2)


def solution(mesh):
    in_specs = (P("day", "col", "row", None), P("day", "col", "row"))
    out_specs = P(("col", "day"), None, "row")
    return jax.shard_map(shards, mesh=mesh, in_specs=in_specs, out_specs=out_specs, check_vma=False)
```

time: 286 us -> 63.6 us (0.22)
  the two profiles are of different devices: /device:TPU:1 before, /device:TPU:53 now
where the time goes in v1:
time: 63.6 us; the launch traced here: 63.3 us
  Pallas kernels  53.8 us (85%)
  local copies, waits for them, and re-layouts  9.47 us (15%)
    pallas_call x1, Pallas kernels, shards(): pl.pallas_call(kernel, out_shape=jax.ShapeDtypeStruct((ROWS, CH), F32), i...  53.8 us
    unnamed x18, local copies, waits for them, and re-layouts  8.73 us

profile of v1, /device:TPU:53, one launch (start us, length us, event | category | flops | bytes accessed | tf_op | source)
XLA Modules:
  0.0 63.3 jit_solution(13663016177205077995)
XLA Ops:
  0.0 0.0 copy-start
  0.0 1.4 %copy-done = bf16[512,1500]{1,0:T(8,128)(2,1)S(1)} copy-done((bf16[512,1500]{1,0:T(8,128)(2,1)S(1)}, bf16[512,1500]{1,0:T(8,128)(2,1)}, u32[]{:S(2)}) %copy-start) | copy-done | bytes 1536024
  1.4 0.0 copy-start.1
  1.4 1.4 %copy-done.1 = bf16[512,1500]{1,0:T(8,128)(2,1)S(1)} copy-done((bf16[512,1500]{1,0:T(8,128)(2,1)S(1)}, bf16[512,1500]{1,0:T(8,128)(2,1)}, u32[]{:S(2)}) %copy-start.1) | copy-done | bytes 1536024
  2.8 0.0 copy-start.2
  2.8 1.1 %copy-done.2 = bf16[1,1,256,1500]{2,3,1,0:T(8,128)(2,1)S(1)} copy-done((bf16[1,1,256,1500]{2,3,1,0:T(8,128)(2,1)S(1)}, bf16[1,1,256,1500]{2,3,1,0:T(8,128)(2,1)}, u32[]{:S(2)}) %copy-start.2) | copy-done | bytes 768024
  3.9 0.0 copy-start.3
  3.9 0.9 %copy-done.3 = bf16[256,256]{1,0:T(8,128)(2,1)S(1)} copy-done((bf16[256,256]{1,0:T(8,128)(2,1)S(1)}, bf16[256,256]{1,0:T(8,128)(2,1)}, u32[]{:S(2)}) %copy-start.3) | copy-done | bytes 131096
  4.8 0.0 copy-start.4
  4.9 0.9 %copy-done.4 = bf16[208,256]{1,0:T(8,128)(2,1)S(1)} copy-done((bf16[208,256]{1,0:T(8,128)(2,1)S(1)}, bf16[208,256]{1,0:T(8,128)(2,1)}, u32[]{:S(2)}) %copy-start.4) | copy-done | bytes 106520
  5.7 0.0 copy-start.5
  5.7 0.9 %copy-done.5 = bf16[208,256]{1,0:T(8,128)(2,1)S(1)} copy-done((bf16[208,256]{1,0:T(8,128)(2,1)S(1)}, bf16[208,256]{1,0:T(8,128)(2,1)}, u32[]{:S(2)}) %copy-start.5) | copy-done | bytes 106520
  6.6 0.0 copy-start.6
  6.6 0.7 %copy-done.6 = bf16[64,16]{1,0:T(8,128)(2,1)S(1)} copy-done((bf16[64,16]{1,0:T(8,128)(2,1)S(1)}, bf16[64,16]{1,0:T(8,128)(2,1)}, u32[]{:S(2)}) %copy-start.6) | copy-done | bytes 2072
  7.4 0.0 copy-start.7
  7.4 0.7 %copy-done.7 = bf16[16,256]{1,0:T(8,128)(2,1)S(1)} copy-done((bf16[16,256]{1,0:T(8,128)(2,1)S(1)}, bf16[16,256]{1,0:T(8,128)(2,1)}, u32[]{:S(2)}) %copy-start.7) | copy-done | bytes 8216
  8.1 0.0 copy-start.8
  8.1 0.7 %copy-done.8 = s32[1,1,256]{2,1,0:T(1,128)S(1)} copy-done((s32[1,1,256]{2,1,0:T(1,128)S(1)}, s32[1,1,256]{2,1,0:T(1,128)}, u32[]{:S(2)}) %copy-start.8) | copy-done | bytes 1048
  8.7 53.8 %shard_map.91 = f32[208,256]{1,0:T(8,128)S(1)} custom-call(bf16[1500,256]{1,0:T(8,128)(2,1)S(1)} %bitcast.7, s32[1,256]{1,0:T(1,128)S(1)} %bitcast.8, bf16[512,1500]{1,0:T(8,128)(2,1)S(1)} %copy-done.1, bf16[512,1500]{1,0:T(8,128)(2,1)S(1)} %copy-done, bf16[256,256]{1,0:T(8,128)(2,1)S(1)} %copy-done.3, bf16[208,256]{1,0:T(8,128)(2,1)S(1)} %copy-done.5, ...), custom_call_target="tpu_custom_call" | custom-call | tf_op jit(solution)/shard_map/pallas_call | solution.py:338
  62.5 0.7 %reshape.3 = f32[51,4,256]{2,1,0:T(4,128)} reshape(f32[204,256]{1,0:T(8,128)S(1)} %bitcast.6) | data formatting | bytes 417792 | tf_op jit(solution)/shard_map/reshape | solution.py:370
Async XLA Ops:
  0.0 1.4 %copy-start = (bf16[512,1500]{1,0:T(8,128)(2,1)S(1)}, bf16[512,1500]{1,0:T(8,128)(2,1)}, u32[]{:S(2)}) copy-start(bf16[512,1500]{1,0:T(8,128)(2,1)} %constant.15.clone.rest) | copy-start | bytes 4608004
  1.4 1.4 %copy-start.1 = (bf16[512,1500]{1,0:T(8,128)(2,1)S(1)}, bf16[512,1500]{1,0:T(8,128)(2,1)}, u32[]{:S(2)}) copy-start(bf16[512,1500]{1,0:T(8,128)(2,1)} %constant.14.clone.high) | copy-start | bytes 4608004
  2.8 1.1 %copy-start.2 = (bf16[1,1,256,1500]{2,3,1,0:T(8,128)(2,1)S(1)}, bf16[1,1,256,1500]{2,3,1,0:T(8,128)(2,1)}, u32[]{:S(2)}) copy-start(bf16[1,1,256,1500]{2,3,1,0:T(8,128)(2,1)} %param.9) | copy-start | bytes 2304004
  3.9 0.9 %copy-start.3 = (bf16[256,256]{1,0:T(8,128)(2,1)S(1)}, bf16[256,256]{1,0:T(8,128)(2,1)}, u32[]{:S(2)}) copy-start(bf16[256,256]{1,0:T(8,128)(2,1)} %constant.16.clone.band) | copy-start | bytes 393220
  4.8 0.9 %copy-start.4 = (bf16[208,256]{1,0:T(8,128)(2,1)S(1)}, bf16[208,256]{1,0:T(8,128)(2,1)}, u32[]{:S(2)}) copy-start(bf16[208,256]{1,0:T(8,128)(2,1)} %constant.18.clone.sine) | copy-start | bytes 319492
  5.7 0.9 %copy-start.5 = (bf16[208,256]{1,0:T(8,128)(2,1)S(1)}, bf16[208,256]{1,0:T(8,128)(2,1)}, u32[]{:S(2)}) copy-start(bf16[208,256]{1,0:T(8,128)(2,1)} %constant.17.clone.cosine) | copy-start | bytes 319492
  6.6 0.7 %copy-start.6 = (bf16[64,16]{1,0:T(8,128)(2,1)S(1)}, bf16[64,16]{1,0:T(8,128)(2,1)}, u32[]{:S(2)}) copy-start(bf16[64,16]{1,0:T(8,128)(2,1)} %constant.19.clone.rep) | copy-start | bytes 6148
  7.4 0.7 %copy-start.7 = (bf16[16,256]{1,0:T(8,128)(2,1)S(1)}, bf16[16,256]{1,0:T(8,128)(2,1)}, u32[]{:S(2)}) copy-start(bf16[16,256]{1,0:T(8,128)(2,1)} %constant.20.clone.pick) | copy-start | bytes 24580
  8.1 0.7 %copy-start.8 = (s32[1,1,256]{2,1,0:T(1,128)S(1)}, s32[1,1,256]{2,1,0:T(1,128)}, u32[]{:S(2)}) copy-start(s32[1,1,256]{2,1,0:T(1,128)} %param.10) | copy-start | bytes 3076

commit v2 on v1

v2 whole, which is shorter than its diff:
```python
import functools
import math

import jax
import jax.numpy as jnp
import ml_dtypes
import numpy as np
from jax import lax
from jax.experimental import pallas as pl
from jax.experimental.pallas import tpu as pltpu
from jax.sharding import PartitionSpec as P

MESH = pl.DeviceIdType.MESH
BF16 = jnp.bfloat16
F32 = jnp.float32

F = 256
LOW = 60
HALF = 64
MAXLAG = 25
LAGS = 2 * MAXLAG + 1
TLEN = 1500
CH = 256
WIN = 8
GROUP = 4
ROWS = 208
TOP = 112
SLANES = F + 128
H = 2
CP = CH // H


def tables():
    k = np.arange(F)
    t = np.arange(TLEN)
    angle = 2.0 * np.pi / TLEN * ((LOW + k)[:, None] * t[None, :] % TLEN)
    twiddle = np.concatenate([np.cos(angle), -np.sin(angle)], axis=0).astype(np.float32)
    high = twiddle.astype(ml_dtypes.bfloat16)
    rest = (twiddle - high.astype(np.float32)).astype(ml_dtypes.bfloat16)
    band = (np.abs(k[:, None] - k[None, :]) <= HALF).astype(ml_dtypes.bfloat16)
    lag = np.arange(LAGS) - MAXLAG
    lag_angle = 2.0 * np.pi / TLEN * ((LOW + k)[None, :] * lag[:, None] % TLEN)
    cosine = np.zeros((ROWS, F), np.float32)
    sine = np.zeros((ROWS, F), np.float32)
    cosine[: GROUP * LAGS] = np.repeat(np.cos(lag_angle), GROUP, axis=0)
    sine[: GROUP * LAGS] = np.repeat(np.sin(lag_angle), GROUP, axis=0)
    rep = np.zeros((64, 16), ml_dtypes.bfloat16)
    for g in range(2):
        for part in range(2):
            for i in range(16):
                rep[g * 32 + part * 16 + i, part * 8 + g * GROUP + i % GROUP] = 1
    pick = np.zeros((16, CH), ml_dtypes.bfloat16)
    for i in range(16):
        pick[i, (i % 8) * 32] = 1
    return (
        high,
        rest,
        band,
        cosine.astype(ml_dtypes.bfloat16),
        sine.astype(ml_dtypes.bfloat16),
        rep,
        pick,
    )


def kernel(
    noise_hbm, keep_hbm, high_hbm, rest_hbm, band_hbm, cosine_hbm, sine_hbm, rep_hbm, pick_hbm, out,
    noise, keep, high, rest, band, cosine, sine, rep, pick, load,
    wall, kept, marks, sown, held, sfin, spread, tmat, inverse, own, near, part, fold_up, fold_down, got_up, got_down,
    w_send, w_recv, k_send, k_recv, s_send, s_recv, t_send, t_recv, d_send, d_recv,
):
    loads = [
        pltpu.make_async_copy(src, dst, load.at[i])
        for i, (src, dst) in enumerate(
            [
                (noise_hbm, noise),
                (keep_hbm, keep),
                (high_hbm, high),
                (rest_hbm, rest),
                (band_hbm, band),
                (pick_hbm, pick),
                (rep_hbm, rep),
                (cosine_hbm, cosine),
                (sine_hbm, sine),
            ]
        )
    ]
    for copy in loads:
        copy.start()

    row, col, day = lax.axis_index("row"), lax.axis_index("col"), lax.axis_index("day")
    z, x = row // 4, row % 4
    y, core = col // 2, col % 2
    side = x % 2
    holder = core == x // 2
    home = jnp.logical_and(holder, y == z)
    away = jnp.logical_not(home)

    def column(step, flip=0):
        return ((y + step) % 4) * 2 + (core + flip) % 2

    upper, lower, far, sibling = column(1), column(3), column(2), column(0, 1)

    def device(r=row, c=col, d=day):
        return (r, c, d)

    def remote(src, dst, send, recv, target):
        return pltpu.make_async_remote_copy(
            src_ref=src, dst_ref=dst, send_sem=send, recv_sem=recv,
            device_id=target, device_id_type=MESH,
        )

    barrier = pltpu.get_barrier_semaphore()

    def greet(target):
        pl.semaphore_signal(barrier, inc=1, device_id=target, device_id_type=MESH)

    for i in range(1, 8):
        greet(device(c=(col + i) % 8))
    for i in (1, 3):
        greet(device(d=(day + i) % 4))
    @pl.when(holder)
    def _():
        for i in range(8):
            if i:
                greet(device(r=4 * y + x, c=(col + i) % 8))
            else:

                @pl.when(away)
                def _():
                    greet(device(r=4 * y + x))

    for e in range(2):

        @pl.when(x != 2 * core + e)
        def _():
            greet(device(r=4 * z + 2 * core + e))

    for copy in loads[:3]:
        copy.wait()
    spectrum = jnp.dot(high[...], noise[...], preferred_element_type=F32)
    loads[3].wait()
    spectrum += jnp.dot(rest[...], noise[...], preferred_element_type=F32)
    real, imag = spectrum[:F], spectrum[F:]
    magnitude = jnp.sqrt(real * real + imag * imag)
    loads[4].wait()
    total = jnp.dot(band[...], magnitude.astype(BF16), preferred_element_type=F32)
    bins = lax.broadcasted_iota(jnp.int32, (F, CH), 0)
    count = jnp.minimum(bins + HALF, F - 1) - jnp.maximum(bins - HALF, 0) + 1
    levels = total / count.astype(F32) + 1e-6
    keep_row = keep[...].astype(F32)
    scale = keep_row / levels
    white = jnp.concatenate([real * scale, imag * scale], axis=0).astype(BF16)
    for h in range(H):
        wall[h, col] = white[:, h * CP : (h + 1) * CP]
    kept[col] = jnp.concatenate(
        [jnp.broadcast_to(keep_row[:, :128], (8, 128)), jnp.broadcast_to(keep_row[:, 128:], (8, 128))]
    ).astype(BF16)
    marks[...] = jnp.zeros_like(marks)

    loads[5].wait()
    picked = lax.dot_general(
        pick[...], white, (((1,), (1,)), ((), ())), preferred_element_type=F32
    )
    lower_half = lax.broadcasted_iota(jnp.int32, (16, F), 0) < 8
    mixed = jnp.where(lower_half, picked[:, :F], picked[:, F:])
    flag = jnp.sum(pick[...].astype(F32) * keep_row, axis=1, keepdims=True)
    message = jnp.concatenate([mixed, jnp.broadcast_to(flag, (16, 128))], axis=1).astype(BF16)
    sown[...] = message

    @pl.when(home)
    def _():
        held[col] = message

    pl.semaphore_wait(barrier, 7 + 2 + 3 + away.astype(jnp.int32) + 3 * holder.astype(jnp.int32))

    def s_copy(k):
        target = device(r=((z + k) % 4) * 4 + x, c=row // 2)
        return remote(sown, held.at[col], s_send.at[k], s_recv.at[col], target)

    def s_each(method):
        for k in (1, 2, 3):
            getattr(s_copy(k), method)()

        @pl.when(away)
        def _():
            getattr(s_copy(0), method)()

    s_each("start")

    def t_copy(i):
        ref = sfin.at[side]
        target = device(r=z * 4 + (x + i) % 4)
        return remote(ref, ref, t_send.at[i - 1], t_recv.at[side], target)

    def s_forward():
        @pl.when(holder)
        def _():
            for w in range(WIN):

                @pl.when(jnp.logical_not(home & (col == w)))
                def _():
                    remote(
                        sown, held.at[w], s_send.at[0], s_recv.at[w], device(c=sibling)
                    ).wait_recv()

            lane = lax.broadcasted_iota(jnp.int32, (16, 128), 1)
            mark = jnp.zeros((16, 128), F32)
            for w in range(WIN):
                sfin[side, w] = held[w, :, 0:F]
                mark = jnp.where(lane == w, held[w, :, F:].astype(F32), mark)
            sfin[side, WIN] = jnp.concatenate([mark, mark], axis=1).astype(BF16)

    def s_spread(e):
        @pl.when(holder & (side == e))
        def _():
            for i in (1, 2, 3):
                t_copy(i).start()

    def s_arrival(e):
        @pl.when(jnp.logical_not(holder & (side == e)))
        def _():
            ref = sfin.at[e]
            remote(ref, ref, t_send.at[0], t_recv.at[e], device(c=sibling)).wait_recv()

    top, bottom = (0, F), (F, F)

    def block(h, w, rows):
        if rows is None:
            return wall.at[h, w]
        return wall.at[h, w, pl.ds(rows[0], rows[1]), :]

    routes = [
        (col, top, upper, lower),
        (col, bottom, lower, upper),
        (col, bottom, upper, lower),
        (col, top, lower, upper),
        (col, None, sibling, sibling),
        (lower, top, upper, far),
        (upper, bottom, lower, far),
        (lower, None, sibling, column(3, 1)),
        (upper, None, sibling, column(1, 1)),
        (far, top, sibling, column(2, 1)),
        (far, bottom, sibling, column(2, 1)),
    ]

    def w_copy(h, index):
        w, rows, target, _ = routes[index]
        ref = block(h, w, rows)
        return remote(ref, ref, w_send.at[h, index], w_recv.at[h, index], device(c=target))

    def w_arrival(h, *indices):
        for index in indices:
            _, rows, _, w = routes[index]
            ref = block(h, w, rows)
            remote(
                ref, ref, w_send.at[h, index], w_recv.at[h, index], device(c=sibling)
            ).wait_recv()

    def w_start(h, *indices):
        for index in indices:
            w_copy(h, index).start()

    def k_copy(i):
        ref = kept.at[col]
        return remote(ref, ref, k_send.at[i - 1], k_recv.at[i - 1], device(c=(col + i) % 8))

    def first_hop(h):
        w_start(h, 0, 1)

    def second_hop(h):
        w_arrival(h, 0)
        w_start(h, 5)
        w_arrival(h, 1)
        w_start(h, 6, 2, 3, 4)

    def third_hop(h):
        w_arrival(h, 2)
        w_start(h, 7)
        w_arrival(h, 3)
        w_start(h, 8)
        w_arrival(h, 5)
        w_start(h, 9)
        w_arrival(h, 6)
        w_start(h, 10)

    def last_hop(h):
        w_arrival(h, 4, 7, 8, 9, 10)

    def spread_sources(e):
        def body(w, carry):
            rows = jnp.dot(rep[...], sfin[e, w], preferred_element_type=F32)
            spread[e, w] = rows.astype(BF16)
            return carry

        lax.fori_loop(0, WIN, body, 0, unroll=4)

    def count_pairs(e):
        rows = jnp.dot(rep[...], sfin[e, WIN, :, 0:128], preferred_element_type=F32)
        pairs = jnp.dot(rows.astype(BF16), marks[...], preferred_element_type=F32)
        for g in range(2):
            floor = jnp.maximum(pairs[32 * g : 32 * g + 16], 1.0)
            inverse[2 * e + g] = (1.0 / math.sqrt(F)) / floor

    def make(d):
        e, g = d // 2, d % 2
        real_rows = pl.ds(pl.multiple_of(32 * g, 32), 16)
        imag_rows = pl.ds(pl.multiple_of(32 * g + 16, 16), 16)

        def body(w, carry):
            s_real = spread[e, w, real_rows, :]
            s_imag = spread[e, w, imag_rows, :]
            at = pl.multiple_of(w * 2 * F, 2 * F)
            for t in range(ROWS // 16):
                rows = slice(16 * t, 16 * t + 16)
                cos_rows, sin_rows = cosine[rows, :], sine[rows, :]
                tmat[d, rows, pl.ds(at, F)] = s_real * cos_rows + s_imag * sin_rows
                tmat[d, rows, pl.ds(at + F, F)] = s_imag * cos_rows - s_real * sin_rows
            return carry

        lax.fori_loop(0, WIN, body, 0)

    def partial(h, d):
        value = jnp.dot(
            tmat[d], wall[h].reshape(WIN * 2 * F, CP), preferred_element_type=F32
        )
        factor = inverse[d, :, h * CP : (h + 1) * CP]
        return (value.reshape(ROWS // 16, 16, CP) * factor[None]).reshape(ROWS, CP)

    up, down, away_day = (day + 1) % 4, (day + 3) % 4, (day + 2) % 4
    head, tail = pl.ds(0, TOP), pl.ds(TOP, ROWS - TOP)

    def d_copy(h, index):
        src, dst, target = [
            (part.at[h, 0, head, :], fold_up.at[h], up),
            (part.at[h, 0, tail, :], fold_down.at[h], down),
            (part.at[h, 1, tail, :], got_up.at[h, tail, :], up),
            (part.at[h, 2, head, :], got_down.at[h, head, :], down),
            (part.at[h, 1, head, :], got_up.at[h, head, :], up),
            (part.at[h, 2, tail, :], got_down.at[h, tail, :], down),
        ][index]
        return remote(src, dst, d_send.at[h, index], d_recv.at[h, index], device(d=target))

    def send_far(h):
        part[h, 0] = partial(h, away_day).astype(BF16)
        d_copy(h, 0).start()
        d_copy(h, 1).start()

    def send_near(h):
        plus = partial(h, up)
        near[h, 0] = plus
        part[h, 1, TOP:, :] = plus[TOP:].astype(BF16)
        minus = partial(h, down)
        near[h, 1] = minus
        part[h, 2, 0:TOP, :] = minus[:TOP].astype(BF16)
        d_copy(h, 0).wait_send()
        d_copy(h, 2).start()
        d_copy(h, 1).wait_send()
        d_copy(h, 3).start()

    def send_folded(h):
        d_copy(h, 0).wait_recv()
        part[h, 1, 0:TOP, :] = (near[h, 0, 0:TOP, :] + fold_up[h].astype(F32)).astype(BF16)
        d_copy(h, 4).start()
        d_copy(h, 1).wait_recv()
        part[h, 2, TOP:, :] = (near[h, 1, TOP:, :] + fold_down[h].astype(F32)).astype(BF16)
        d_copy(h, 5).start()

    def finish(h):
        for index in (2, 3, 4, 5):
            d_copy(h, index).wait_recv()
        result = own[h] + got_up[h].astype(F32) + got_down[h].astype(F32)
        out[:, h * CP : (h + 1) * CP] = result

    def k_arrival():
        for i in range(1, 8):
            ref = kept.at[(col + 8 - i) % 8]
            remote(ref, ref, k_send.at[i - 1], k_recv.at[i - 1], device(c=sibling)).wait_recv()
        rows = [
            jnp.concatenate([kept[w, 0:1, :], kept[w, 8:9, :]], axis=1).astype(F32)
            for w in range(WIN)
        ]
        marks[0:16, :] = jnp.concatenate(rows + [jnp.zeros((8, CH), F32)]).astype(BF16)

    first_side = away_day // 2
    first_hop(0)
    for i in range(1, 8):
        k_copy(i).start()
    s_forward()
    s_spread(first_side)
    second_hop(0)
    s_spread(1 - first_side)
    for copy in loads[6:]:
        copy.wait()
    s_arrival(first_side)
    first_hop(1)
    spread_sources(first_side)
    k_arrival()
    count_pairs(first_side)
    make(away_day)
    third_hop(0)
    last_hop(0)
    send_far(0)
    second_hop(1)
    s_arrival(1 - first_side)
    spread_sources(1 - first_side)
    count_pairs(1 - first_side)
    make(up)
    make(down)
    send_near(0)
    third_hop(1)
    send_folded(0)
    last_hop(1)
    send_far(1)
    make(day)
    send_near(1)
    own[0] = partial(0, day)
    send_folded(1)
    own[1] = partial(1, day)
    finish(0)
    finish(1)

    s_each("wait_send")

    @pl.when(holder)
    def _():
        for i in (1, 2, 3):
            t_copy(i).wait_send()

    for i in range(1, 8):
        k_copy(i).wait_send()
    for h in range(H):
        for index in range(11):
            w_copy(h, index).wait_send()
        for index in (2, 3, 4, 5):
            d_copy(h, index).wait_send()


def shards(noise, keep):
    samples = noise[0, 0].T
    consts = tables()
    dma = pltpu.SemaphoreType.DMA
    result = pl.pallas_call(
        kernel,
        out_shape=jax.ShapeDtypeStruct((ROWS, CH), F32),
        in_specs=[
            pl.BlockSpec(memory_space=pltpu.HBM)
            for i in range(2 + len(consts))
        ],
        out_specs=pl.BlockSpec(memory_space=pltpu.VMEM),
        scratch_shapes=[
            pltpu.VMEM(samples.shape, BF16),
            pltpu.VMEM((1, CH), jnp.int32),
            *[pltpu.VMEM(c.shape, BF16) for c in consts],
            dma((2 + len(consts),)),
            pltpu.VMEM((H, WIN, 2 * F, CP), BF16),
            pltpu.VMEM((WIN, 16, 128), BF16),
            pltpu.VMEM((128, CH), BF16),
            pltpu.VMEM((16, SLANES), BF16),
            pltpu.VMEM((WIN, 16, SLANES), BF16),
            pltpu.VMEM((2, WIN + 1, 16, F), BF16),
            pltpu.VMEM((2, WIN, 64, F), BF16),
            pltpu.VMEM((4, ROWS, WIN * 2 * F), BF16),
            pltpu.VMEM((4, 16, CH), F32),
            pltpu.VMEM((H, ROWS, CP), F32),
            pltpu.VMEM((H, 2, ROWS, CP), F32),
            pltpu.VMEM((H, 3, ROWS, CP), BF16),
            pltpu.VMEM((H, TOP, CP), BF16),
            pltpu.VMEM((H, ROWS - TOP, CP), BF16),
            pltpu.VMEM((H, ROWS, CP), BF16),
            pltpu.VMEM((H, ROWS, CP), BF16),
            dma((H, 11)),
            dma((H, 11)),
            dma((7,)),
            dma((7,)),
            dma((4,)),
            dma((WIN,)),
            dma((3,)),
            dma((2,)),
            dma((H, 6)),
            dma((H, 6)),
        ],
        compiler_params=pltpu.CompilerParams(
            collective_id=0, has_side_effects=True, vmem_limit_bytes=60 * 1024 * 1024
        ),
    )(samples, keep[0], *[jnp.asarray(c) for c in consts])
    return result[: GROUP * LAGS].reshape(LAGS, GROUP, CH).transpose(1, 0, 2)


def solution(mesh):
    in_specs = (P("day", "col", "row", None), P("day", "col", "row"))
    out_specs = P(("col", "day"), None, "row")
    return jax.shard_map(shards, mesh=mesh, in_specs=in_specs, out_specs=out_specs, check_vma=False)
```

time: 63.6 us -> 49.5 us (0.78)
  the two profiles are of different devices: /device:TPU:53 before, /device:TPU:24 now
where the time goes in v2:
time: 49.5 us; the launch traced here: 49.3 us
  Pallas kernels  47.7 us (96%)
  local copies, waits for them, and re-layouts  1.67 us (3%)
    pallas_call x1, Pallas kernels, shards(): pl.pallas_call(kernel, out_shape=jax.ShapeDtypeStruct((ROWS, CH), F32), i...  47.7 us
    reshape x1, local copies, waits for them, and re-layouts, shards(): return result[:GROUP * LAGS].reshape(LAGS, GROUP, CH).transpose(1, 0, 2)  1.67 us

profile of v2, /device:TPU:24, one launch (start us, length us, event | category | flops | bytes accessed | tf_op | source)
XLA Modules:
  0.0 49.3 jit_solution(7804791334023100173)
XLA Ops:
  0.0 47.7 %shard_map.91 = f32[208,256]{1,0:T(8,128)} custom-call(bf16[1500,256]{1,0:T(8,128)(2,1)} %bitcast.7, s32[1,256]{1,0:T(1,128)} %bitcast.8, bf16[512,1500]{1,0:T(8,128)(2,1)} %constant.14.clone.high_hbm, bf16[512,1500]{1,0:T(8,128)(2,1)} %constant.15.clone.rest_hbm, bf16[256,256]{1,0:T(8,128)(2,1)} %constant.16.clone.band_hbm, ...), custom_call_target="tpu_custom_call" | custom-call | tf_op jit(solution)/shard_map/pallas_call | solution.py:443
  47.7 1.7 %reshape.3 = f32[51,4,256]{2,1,0:T(4,128)} reshape(f32[204,256]{1,0:T(8,128)} %bitcast.6) | data formatting | bytes 417792 | tf_op jit(solution)/shard_map/reshape | solution.py:487

commit v3 on v2

--- a/solution.py
+++ b/solution.py
@@ -23,10 +23,13 @@
 CH = 256
 WIN = 8
 GROUP = 4
-ROWS = 208
-TOP = 112
+HALFRANK = 16
+RANK = 2 * HALFRANK
+ROWS = GROUP * RANK
+TOP = ROWS // 2
+OUT = 208
 SLANES = F + 128
-H = 2
+H = 1
 CP = CH // H
 
 
@@ -40,10 +43,18 @@
     band = (np.abs(k[:, None] - k[None, :]) <= HALF).astype(ml_dtypes.bfloat16)
     lag = np.arange(LAGS) - MAXLAG
     lag_angle = 2.0 * np.pi / TLEN * ((LOW + k)[None, :] * lag[:, None] % TLEN)
-    cosine = np.zeros((ROWS, F), np.float32)
-    sine = np.zeros((ROWS, F), np.float32)
-    cosine[: GROUP * LAGS] = np.repeat(np.cos(lag_angle), GROUP, axis=0)
-    sine[: GROUP * LAGS] = np.repeat(np.sin(lag_angle), GROUP, axis=0)
+    back, basis = [], []
+    for part in (np.cos(lag_angle), -np.sin(lag_angle)):
+        left, size, right = np.linalg.svd(part, full_matrices=False)
+        left, size, right = left[:, :HALFRANK], size[:HALFRANK], right[:HALFRANK]
+        back.append(left * size / 16.0)
+        basis.append(right * 16.0)
+    basis = np.repeat(np.concatenate(basis), GROUP, axis=0).astype(ml_dtypes.bfloat16)
+    synth = np.zeros((OUT, ROWS), np.float32)
+    synth[: GROUP * LAGS] = np.kron(np.concatenate(back, axis=1), np.eye(GROUP))
+    synth_high = synth.astype(ml_dtypes.bfloat16)
+    synth_rest = (synth - synth_high.astype(np.float32)).astype(ml_dtypes.bfloat16)
+    synth = np.concatenate([synth_high, synth_high, synth_rest], axis=1)
     rep = np.zeros((64, 16), ml_dtypes.bfloat16)
     for g in range(2):
         for part in range(2):
@@ -56,16 +67,16 @@
         high,
         rest,
         band,
-        cosine.astype(ml_dtypes.bfloat16),
-        sine.astype(ml_dtypes.bfloat16),
+        basis,
+        synth,
         rep,
         pick,
     )
 
 
 def kernel(
-    noise_hbm, keep_hbm, high_hbm, rest_hbm, band_hbm, cosine_hbm, sine_hbm, rep_hbm, pick_hbm, out,
-    noise, keep, high, rest, band, cosine, sine, rep, pick, load,
+    noise_hbm, keep_hbm, high_hbm, rest_hbm, band_hbm, basis_hbm, synth_hbm, rep_hbm, pick_hbm, out,
+    noise, keep, high, rest, band, basis, synth, rep, pick, load,
     wall, kept, marks, sown, held, sfin, spread, tmat, inverse, own, near, part, fold_up, fold_down, got_up, got_down,
     w_send, w_recv, k_send, k_recv, s_send, s_recv, t_send, t_recv, d_send, d_recv,
 ):
@@ -80,8 +91,8 @@
                 (band_hbm, band),
                 (pick_hbm, pick),
                 (rep_hbm, rep),
-                (cosine_hbm, cosine),
-                (sine_hbm, sine),
+                (basis_hbm, basis),
+                (synth_hbm, synth),
             ]
         )
     ]
@@ -141,39 +152,23 @@
     spectrum = jnp.dot(high[...], noise[...], preferred_element_type=F32)
     loads[3].wait()
     spectrum += jnp.dot(rest[...], noise[...], preferred_element_type=F32)
-    real, imag = spectrum[:F], spectrum[F:]
-    magnitude = jnp.sqrt(real * real + imag * imag)
     loads[4].wait()
-    total = jnp.dot(band[...], magnitude.astype(BF16), preferred_element_type=F32)
-    bins = lax.broadcasted_iota(jnp.int32, (F, CH), 0)
+    keep_row = keep[...].astype(F32)
+    bins = lax.broadcasted_iota(jnp.int32, (F, CP), 0)
     count = jnp.minimum(bins + HALF, F - 1) - jnp.maximum(bins - HALF, 0) + 1
-    levels = total / count.astype(F32) + 1e-6
-    keep_row = keep[...].astype(F32)
-    scale = keep_row / levels
-    white = jnp.concatenate([real * scale, imag * scale], axis=0).astype(BF16)
-    for h in range(H):
-        wall[h, col] = white[:, h * CP : (h + 1) * CP]
-    kept[col] = jnp.concatenate(
-        [jnp.broadcast_to(keep_row[:, :128], (8, 128)), jnp.broadcast_to(keep_row[:, 128:], (8, 128))]
-    ).astype(BF16)
-    marks[...] = jnp.zeros_like(marks)
-
-    loads[5].wait()
-    picked = lax.dot_general(
-        pick[...], white, (((1,), (1,)), ((), ())), preferred_element_type=F32
-    )
-    lower_half = lax.broadcasted_iota(jnp.int32, (16, F), 0) < 8
-    mixed = jnp.where(lower_half, picked[:, :F], picked[:, F:])
-    flag = jnp.sum(pick[...].astype(F32) * keep_row, axis=1, keepdims=True)
-    message = jnp.concatenate([mixed, jnp.broadcast_to(flag, (16, 128))], axis=1).astype(BF16)
-    sown[...] = message
-
-    @pl.when(home)
-    def _():
-        held[col] = message
-
-    pl.semaphore_wait(barrier, 7 + 2 + 3 + away.astype(jnp.int32) + 3 * holder.astype(jnp.int32))
-
+    weight = 1.0 / count.astype(F32)
+
+    def whiten(h):
+        cut = slice(h * CP, (h + 1) * CP)
+        real, imag = spectrum[:F, cut], spectrum[F:, cut]
+        magnitude = jnp.sqrt(real * real + imag * imag)
+        total = jnp.dot(band[...], magnitude.astype(BF16), preferred_element_type=F32)
+        scale = keep_row[:, cut] / (total * weight + 1e-6)
+        white = jnp.concatenate([real * scale, imag * scale], axis=0).astype(BF16)
+        wall[h, col] = white
+        return white
+
+    white = [whiten(0)]
     def s_copy(k):
         target = device(r=((z + k) % 4) * 4 + x, c=row // 2)
         return remote(sown, held.at[col], s_send.at[k], s_recv.at[col], target)
@@ -185,8 +180,6 @@
         @pl.when(away)
         def _():
             getattr(s_copy(0), method)()
-
-    s_each("start")
 
     def t_copy(i):
         ref = sfin.at[side]
@@ -214,7 +207,7 @@
     def s_spread(e):
         @pl.when(holder & (side == e))
         def _():
-            for i in (1, 2, 3):
+            for i in (2, 1, 3):
                 t_copy(i).start()
 
     def s_arrival(e):
@@ -268,17 +261,22 @@
     def first_hop(h):
         w_start(h, 0, 1)
 
+    def rest_hop(h):
+        w_start(h, 2, 3, 4)
+
     def second_hop(h):
         w_arrival(h, 0)
         w_start(h, 5)
         w_arrival(h, 1)
-        w_start(h, 6, 2, 3, 4)
+        w_start(h, 6)
 
     def third_hop(h):
         w_arrival(h, 2)
         w_start(h, 7)
         w_arrival(h, 3)
         w_start(h, 8)
+
+    def fourth_hop(h):
         w_arrival(h, 5)
         w_start(h, 9)
         w_arrival(h, 6)
@@ -302,7 +300,7 @@
             floor = jnp.maximum(pairs[32 * g : 32 * g + 16], 1.0)
             inverse[2 * e + g] = (1.0 / math.sqrt(F)) / floor
 
-    def make(d):
+    def make(slot, d):
         e, g = d // 2, d % 2
         real_rows = pl.ds(pl.multiple_of(32 * g, 32), 16)
         imag_rows = pl.ds(pl.multiple_of(32 * g + 16, 16), 16)
@@ -313,16 +311,17 @@
             at = pl.multiple_of(w * 2 * F, 2 * F)
             for t in range(ROWS // 16):
                 rows = slice(16 * t, 16 * t + 16)
-                cos_rows, sin_rows = cosine[rows, :], sine[rows, :]
-                tmat[d, rows, pl.ds(at, F)] = s_real * cos_rows + s_imag * sin_rows
-                tmat[d, rows, pl.ds(at + F, F)] = s_imag * cos_rows - s_real * sin_rows
+                table = basis[rows, :]
+                first, second = (s_real, s_imag) if 2 * t < ROWS // 16 else (-s_imag, s_real)
+                tmat[slot, rows, pl.ds(at, F)] = first * table
+                tmat[slot, rows, pl.ds(at + F, F)] = second * table
             return carry
 
         lax.fori_loop(0, WIN, body, 0)
 
-    def partial(h, d):
+    def partial(h, slot, d):
         value = jnp.dot(
-            tmat[d], wall[h].reshape(WIN * 2 * F, CP), preferred_element_type=F32
+            tmat[slot], wall[h].reshape(WIN * 2 * F, CP), preferred_element_type=F32
         )
         factor = inverse[d, :, h * CP : (h + 1) * CP]
         return (value.reshape(ROWS // 16, 16, CP) * factor[None]).reshape(ROWS, CP)
@@ -342,20 +341,24 @@
         return remote(src, dst, d_send.at[h, index], d_recv.at[h, index], device(d=target))
 
     def send_far(h):
-        part[h, 0] = partial(h, away_day).astype(BF16)
+        part[h, 0] = partial(h, 0, away_day).astype(BF16)
         d_copy(h, 0).start()
         d_copy(h, 1).start()
 
-    def send_near(h):
-        plus = partial(h, up)
+    def compute_near(h):
+        plus = partial(h, 1, up)
         near[h, 0] = plus
         part[h, 1, TOP:, :] = plus[TOP:].astype(BF16)
-        minus = partial(h, down)
+        minus = partial(h, 2, down)
         near[h, 1] = minus
         part[h, 2, 0:TOP, :] = minus[:TOP].astype(BF16)
+
+    def drain_far(h):
         d_copy(h, 0).wait_send()
+        d_copy(h, 1).wait_send()
+
+    def send_near(h):
         d_copy(h, 2).start()
-        d_copy(h, 1).wait_send()
         d_copy(h, 3).start()
 
     def send_folded(h):
@@ -370,7 +373,13 @@
         for index in (2, 3, 4, 5):
             d_copy(h, index).wait_recv()
         result = own[h] + got_up[h].astype(F32) + got_down[h].astype(F32)
-        out[:, h * CP : (h + 1) * CP] = result
+        high_part = result.astype(BF16)
+        rest_part = (result - high_part.astype(F32)).astype(BF16)
+        out[:, h * CP : (h + 1) * CP] = jnp.dot(
+            synth[...],
+            jnp.concatenate([high_part, rest_part, high_part]),
+            preferred_element_type=F32,
+        )
 
     def k_arrival():
         for i in range(1, 8):
@@ -383,42 +392,62 @@
         marks[0:16, :] = jnp.concatenate(rows + [jnp.zeros((8, CH), F32)]).astype(BF16)
 
     first_side = away_day // 2
+    pl.semaphore_wait(barrier, 7 + 2 + 3 + away.astype(jnp.int32) + 3 * holder.astype(jnp.int32))
     first_hop(0)
+    kept[col] = jnp.concatenate(
+        [jnp.broadcast_to(keep_row[:, :128], (8, 128)), jnp.broadcast_to(keep_row[:, 128:], (8, 128))]
+    ).astype(BF16)
+    marks[...] = jnp.zeros_like(marks)
+
+    loads[5].wait()
+    picked = jnp.zeros((16, 2 * F), F32)
+    for h in range(H):
+        picked += lax.dot_general(
+            pick[:, h * CP : (h + 1) * CP],
+            white[h],
+            (((1,), (1,)), ((), ())),
+            preferred_element_type=F32,
+        )
+    lower_half = lax.broadcasted_iota(jnp.int32, (16, F), 0) < 8
+    mixed = jnp.where(lower_half, picked[:, :F], picked[:, F:])
+    flag = jnp.sum(pick[...].astype(F32) * keep_row, axis=1, keepdims=True)
+    message = jnp.concatenate([mixed, jnp.broadcast_to(flag, (16, 128))], axis=1).astype(BF16)
+    sown[...] = message
+
+    @pl.when(home)
+    def _():
+        held[col] = message
+    s_each("start")
+    rest_hop(0)
     for i in range(1, 8):
         k_copy(i).start()
+    second_hop(0)
     s_forward()
     s_spread(first_side)
-    second_hop(0)
     s_spread(1 - first_side)
+    third_hop(0)
     for copy in loads[6:]:
         copy.wait()
+    k_arrival()
     s_arrival(first_side)
-    first_hop(1)
     spread_sources(first_side)
-    k_arrival()
+    make(0, away_day)
+    fourth_hop(0)
+    s_arrival(1 - first_side)
+    spread_sources(1 - first_side)
     count_pairs(first_side)
-    make(away_day)
-    third_hop(0)
+    count_pairs(1 - first_side)
+    make(1, up)
+    make(2, down)
     last_hop(0)
     send_far(0)
-    second_hop(1)
-    s_arrival(1 - first_side)
-    spread_sources(1 - first_side)
-    count_pairs(1 - first_side)
-    make(up)
-    make(down)
+    compute_near(0)
+    drain_far(0)
     send_near(0)
-    third_hop(1)
+    make(3, day)
+    own[0] = partial(0, 3, day)
     send_folded(0)
-    last_hop(1)
-    send_far(1)
-    make(day)
-    send_near(1)
-    own[0] = partial(0, day)
-    send_folded(1)
-    own[1] = partial(1, day)
     finish(0)
-    finish(1)
 
     s_each("wait_send")
 
@@ -442,7 +471,7 @@
     dma = pltpu.SemaphoreType.DMA
     result = pl.pallas_call(
         kernel,
-        out_shape=jax.ShapeDtypeStruct((ROWS, CH), F32),
+        out_shape=jax.ShapeDtypeStruct((OUT, CH), F32),
         in_specs=[
             pl.BlockSpec(memory_space=pltpu.HBM)
             for i in range(2 + len(consts))

time: 49.5 us -> 44.1 us (0.89)
  the two profiles are of different devices: /device:TPU:24 before, /device:TPU:1 now
where the time goes in v3:
time: 44.1 us; the launch traced here: 43.9 us
  Pallas kernels  42.2 us (96%)
  local copies, waits for them, and re-layouts  1.67 us (4%)
    pallas_call x1, Pallas kernels, shards(): pl.pallas_call(kernel, out_shape=jax.ShapeDtypeStruct((OUT, CH), F32), in...  42.2 us
    reshape x1, local copies, waits for them, and re-layouts, shards(): return result[:GROUP * LAGS].reshape(LAGS, GROUP, CH).transpose(1, 0, 2)  1.67 us

profile of v3, /device:TPU:1, one launch (start us, length us, event | category | flops | bytes accessed | tf_op | source)
XLA Modules:
  0.0 43.9 jit_solution(17339052133606433116)
XLA Ops:
  0.0 42.2 %shard_map.91 = f32[208,256]{1,0:T(8,128)} custom-call(bf16[1500,256]{1,0:T(8,128)(2,1)} %bitcast.7, s32[1,256]{1,0:T(1,128)} %bitcast.8, bf16[512,1500]{1,0:T(8,128)(2,1)} %constant.14.clone.high_hbm, bf16[512,1500]{1,0:T(8,128)(2,1)} %constant.15.clone.rest_hbm, bf16[256,256]{1,0:T(8,128)(2,1)} %constant.16.clone.band_hbm, ...), custom_call_target="tpu_custom_call" | custom-call | tf_op jit(solution)/shard_map/pallas_call | solution.py:472
  42.3 1.7 %reshape.3 = f32[51,4,256]{2,1,0:T(4,128)} reshape(f32[204,256]{1,0:T(8,128)} %bitcast.6) | data formatting | bytes 417792 | tf_op jit(solution)/shard_map/reshape | solution.py:516

commit v4 on v3

--- a/solution.py
+++ b/solution.py
@@ -31,6 +31,8 @@
 SLANES = F + 128
 H = 1
 CP = CH // H
+PARTS = 2
+DP = CH // PARTS
 
 
 def tables():
@@ -319,12 +321,13 @@
 
         lax.fori_loop(0, WIN, body, 0)
 
-    def partial(h, slot, d):
+    def partial(p, slot, d):
+        cut = slice(p * DP, (p + 1) * DP)
         value = jnp.dot(
-            tmat[slot], wall[h].reshape(WIN * 2 * F, CP), preferred_element_type=F32
+            tmat[slot], wall[0, :, :, cut].reshape(WIN * 2 * F, DP), preferred_element_type=F32
         )
-        factor = inverse[d, :, h * CP : (h + 1) * CP]
-        return (value.reshape(ROWS // 16, 16, CP) * factor[None]).reshape(ROWS, CP)
+        factor = inverse[d, :, cut]
+        return (value.reshape(ROWS // 16, 16, DP) * factor[None]).reshape(ROWS, DP)
 
     up, down, away_day = (day + 1) % 4, (day + 3) % 4, (day + 2) % 4
     head, tail = pl.ds(0, TOP), pl.ds(TOP, ROWS - TOP)
@@ -353,10 +356,6 @@
         near[h, 1] = minus
         part[h, 2, 0:TOP, :] = minus[:TOP].astype(BF16)
 
-    def drain_far(h):
-        d_copy(h, 0).wait_send()
-        d_copy(h, 1).wait_send()
-
     def send_near(h):
         d_copy(h, 2).start()
         d_copy(h, 3).start()
@@ -375,7 +374,7 @@
         result = own[h] + got_up[h].astype(F32) + got_down[h].astype(F32)
         high_part = result.astype(BF16)
         rest_part = (result - high_part.astype(F32)).astype(BF16)
-        out[:, h * CP : (h + 1) * CP] = jnp.dot(
+        out[:, h * DP : (h + 1) * DP] = jnp.dot(
             synth[...],
             jnp.concatenate([high_part, rest_part, high_part]),
             preferred_element_type=F32,
@@ -418,9 +417,9 @@
     def _():
         held[col] = message
     s_each("start")
-    rest_hop(0)
     for i in range(1, 8):
         k_copy(i).start()
+    rest_hop(0)
     second_hop(0)
     s_forward()
     s_spread(first_side)
@@ -441,13 +440,18 @@
     make(2, down)
     last_hop(0)
     send_far(0)
+    send_far(1)
     compute_near(0)
-    drain_far(0)
     send_near(0)
+    compute_near(1)
+    send_near(1)
     make(3, day)
     own[0] = partial(0, 3, day)
+    own[1] = partial(1, 3, day)
     send_folded(0)
+    send_folded(1)
     finish(0)
+    finish(1)
 
     s_each("wait_send")
 
@@ -461,8 +465,9 @@
     for h in range(H):
         for index in range(11):
             w_copy(h, index).wait_send()
-        for index in (2, 3, 4, 5):
-            d_copy(h, index).wait_send()
+    for p in range(PARTS):
+        for index in range(6):
+            d_copy(p, index).wait_send()
 
 
 def shards(noise, keep):
@@ -491,13 +496,13 @@
             pltpu.VMEM((2, WIN, 64, F), BF16),
             pltpu.VMEM((4, ROWS, WIN * 2 * F), BF16),
             pltpu.VMEM((4, 16, CH), F32),
-            pltpu.VMEM((H, ROWS, CP), F32),
-            pltpu.VMEM((H, 2, ROWS, CP), F32),
-            pltpu.VMEM((H, 3, ROWS, CP), BF16),
-            pltpu.VMEM((H, TOP, CP), BF16),
-            pltpu.VMEM((H, ROWS - TOP, CP), BF16),
-            pltpu.VMEM((H, ROWS, CP), BF16),
-            pltpu.VMEM((H, ROWS, CP), BF16),
+            pltpu.VMEM((PARTS, ROWS, DP), F32),
+            pltpu.VMEM((PARTS, 2, ROWS, DP), F32),
+            pltpu.VMEM((PARTS, 3, ROWS, DP), BF16),
+            pltpu.VMEM((PARTS, TOP, DP), BF16),
+            pltpu.VMEM((PARTS, ROWS - TOP, DP), BF16),
+            pltpu.VMEM((PARTS, ROWS, DP), BF16),
+            pltpu.VMEM((PARTS, ROWS, DP), BF16),
             dma((H, 11)),
             dma((H, 11)),
             dma((7,)),
@@ -506,8 +511,8 @@
             dma((WIN,)),
             dma((3,)),
             dma((2,)),
-            dma((H, 6)),
-            dma((H, 6)),
+            dma((PARTS, 6)),
+            dma((PARTS, 6)),
         ],
         compiler_params=pltpu.CompilerParams(
             collective_id=0, has_side_effects=True, vmem_limit_bytes=60 * 1024 * 1024

time: 44.1 us -> 43.2 us (0.980)
  Pallas kernels: 42.2 us -> 41.4 us
    pallas_call x1, Pallas kernels: 42.2 us -> 41.4 us  [shards(): pl.pallas_call(kernel, out_shape=jax.ShapeDtypeStruct((OUT, CH), F32), in...]
where the time goes in v4:
time: 43.2 us; the launch traced here: 43.1 us
  Pallas kernels  41.4 us (96%)
  local copies, waits for them, and re-layouts  1.67 us (4%)
    pallas_call x1, Pallas kernels, shards(): pl.pallas_call(kernel, out_shape=jax.ShapeDtypeStruct((OUT, CH), F32), in...  41.4 us
    reshape x1, local copies, waits for them, and re-layouts, shards(): return result[:GROUP * LAGS].reshape(LAGS, GROUP, CH).transpose(1, 0, 2)  1.67 us

profile of v4, /device:TPU:1, one launch (start us, length us, event | category | flops | bytes accessed | tf_op | source)
XLA Modules:
  0.0 43.1 jit_solution(15875404070158528256)
XLA Ops:
  0.0 41.4 %shard_map.91 = f32[208,256]{1,0:T(8,128)} custom-call(bf16[1500,256]{1,0:T(8,128)(2,1)} %bitcast.7, s32[1,256]{1,0:T(1,128)} %bitcast.8, bf16[512,1500]{1,0:T(8,128)(2,1)} %constant.14.clone.high_hbm, bf16[512,1500]{1,0:T(8,128)(2,1)} %constant.15.clone.rest_hbm, bf16[256,256]{1,0:T(8,128)(2,1)} %constant.16.clone.band_hbm, ...), custom_call_target="tpu_custom_call" | custom-call | tf_op jit(solution)/shard_map/pallas_call | solution.py:477
  41.4 1.7 %reshape.3 = f32[51,4,256]{2,1,0:T(4,128)} reshape(f32[204,256]{1,0:T(8,128)} %bitcast.6) | data formatting | bytes 417792 | tf_op jit(solution)/shard_map/reshape | solution.py:521

commit v5 on v4

--- a/solution.py
+++ b/solution.py
@@ -56,7 +56,11 @@
     synth[: GROUP * LAGS] = np.kron(np.concatenate(back, axis=1), np.eye(GROUP))
     synth_high = synth.astype(ml_dtypes.bfloat16)
     synth_rest = (synth - synth_high.astype(np.float32)).astype(ml_dtypes.bfloat16)
-    synth = np.concatenate([synth_high, synth_high, synth_rest], axis=1)
+    terms = np.concatenate([synth_high, synth_high, synth_rest], axis=1)
+    synth = np.zeros((LAGS, PARTS, GROUP, PARTS, terms.shape[1]), terms.dtype)
+    for p in range(PARTS):
+        synth[:, p, :, p] = terms[: GROUP * LAGS].reshape(LAGS, GROUP, -1)
+    synth = synth.reshape(LAGS * PARTS * GROUP, -1)
     rep = np.zeros((64, 16), ml_dtypes.bfloat16)
     for g in range(2):
         for part in range(2):
@@ -374,11 +378,7 @@
         result = own[h] + got_up[h].astype(F32) + got_down[h].astype(F32)
         high_part = result.astype(BF16)
         rest_part = (result - high_part.astype(F32)).astype(BF16)
-        out[:, h * DP : (h + 1) * DP] = jnp.dot(
-            synth[...],
-            jnp.concatenate([high_part, rest_part, high_part]),
-            preferred_element_type=F32,
-        )
+        return [high_part, rest_part, high_part]
 
     def k_arrival():
         for i in range(1, 8):
@@ -423,24 +423,24 @@
     second_hop(0)
     s_forward()
     s_spread(first_side)
+    third_hop(0)
     s_spread(1 - first_side)
-    third_hop(0)
     for copy in loads[6:]:
         copy.wait()
+    fourth_hop(0)
     k_arrival()
     s_arrival(first_side)
     spread_sources(first_side)
     make(0, away_day)
-    fourth_hop(0)
+    count_pairs(first_side)
+    last_hop(0)
+    send_far(0)
+    send_far(1)
     s_arrival(1 - first_side)
     spread_sources(1 - first_side)
-    count_pairs(first_side)
     count_pairs(1 - first_side)
     make(1, up)
     make(2, down)
-    last_hop(0)
-    send_far(0)
-    send_far(1)
     compute_near(0)
     send_near(0)
     compute_near(1)
@@ -450,8 +450,8 @@
     own[1] = partial(1, 3, day)
     send_folded(0)
     send_folded(1)
-    finish(0)
-    finish(1)
+    terms = finish(0) + finish(1)
+    out[...] = jnp.dot(synth[...], jnp.concatenate(terms), preferred_element_type=F32)
 
     s_each("wait_send")
 
@@ -476,7 +476,7 @@
     dma = pltpu.SemaphoreType.DMA
     result = pl.pallas_call(
         kernel,
-        out_shape=jax.ShapeDtypeStruct((OUT, CH), F32),
+        out_shape=jax.ShapeDtypeStruct((LAGS * PARTS * GROUP, DP), F32),
         in_specs=[
             pl.BlockSpec(memory_space=pltpu.HBM)
             for i in range(2 + len(consts))
@@ -518,7 +518,7 @@
             collective_id=0, has_side_effects=True, vmem_limit_bytes=60 * 1024 * 1024
         ),
     )(samples, keep[0], *[jnp.asarray(c) for c in consts])
-    return result[: GROUP * LAGS].reshape(LAGS, GROUP, CH).transpose(1, 0, 2)
+    return result.reshape(LAGS, PARTS, GROUP, DP).transpose(2, 0, 1, 3).reshape(GROUP, LAGS, CH)
 
 
 def solution(mesh):

time: 43.2 us -> 42.8 us (level)
    reshape x1 -> x0, local copies, waits for them, and re-layouts: 1.67 us -> none  [shards(): return result[:GROUP * LAGS].reshape(LAGS, GROUP, CH).transpose(1, 0, 2)]
    unnamed x0 -> x1, local copies, waits for them, and re-layouts: none -> 1.63 us
where the time goes in v5:
time: 42.8 us; the launch traced here: 42.6 us
  Pallas kernels  41 us (96%)
  local copies, waits for them, and re-layouts  1.63 us (4%)
    pallas_call x1, Pallas kernels, shards(): pl.pallas_call(kernel, out_shape=jax.ShapeDtypeStruct((LAGS * PARTS * GRO...  41 us
    unnamed x1, local copies, waits for them, and re-layouts  1.63 us

profile of v5, /device:TPU:1, one launch (start us, length us, event | category | flops | bytes accessed | tf_op | source)
XLA Modules:
  0.0 42.6 jit_solution(11327023057660043037)
XLA Ops:
  0.0 41.0 %shard_map.91 = f32[408,128]{1,0:T(8,128)} custom-call(bf16[1500,256]{1,0:T(8,128)(2,1)} %bitcast.10, s32[1,256]{1,0:T(1,128)} %bitcast.11, bf16[512,1500]{1,0:T(8,128)(2,1)} %constant.14.clone.high_hbm, bf16[512,1500]{1,0:T(8,128)(2,1)} %constant.15.clone.rest_hbm, bf16[256,256]{1,0:T(8,128)(2,1)} %constant.16.clone.band_hbm, ...), custom_call_target="tpu_custom_call" | custom-call | tf_op jit(solution)/shard_map/pallas_call | solution.py:477
  41.0 1.6 %copy.12 = f32[4,51,256]{2,0,1:T(4,128)} copy(f32[4,51,256]{2,0,1:T(4,128)} %bitcast.9) | data formatting | bytes 417792

commit v6 on v5

--- a/solution.py
+++ b/solution.py
@@ -102,7 +102,7 @@
             ]
         )
     ]
-    for copy in loads:
+    for copy in loads[:3]:
         copy.start()
 
     row, col, day = lax.axis_index("row"), lax.axis_index("col"), lax.axis_index("day")
@@ -153,6 +153,8 @@
         def _():
             greet(device(r=4 * z + 2 * core + e))
 
+    for copy in loads[3:]:
+        copy.start()
     for copy in loads[:3]:
         copy.wait()
     spectrum = jnp.dot(high[...], noise[...], preferred_element_type=F32)

time: 42.8 us -> 42.5 us (level)
  no operation moved by 1% of the time
where the time goes in v6:
time: 42.5 us; the launch traced here: 42.4 us
  Pallas kernels  40.7 us (96%)
  local copies, waits for them, and re-layouts  1.63 us (4%)
    pallas_call x1, Pallas kernels, shards(): pl.pallas_call(kernel, out_shape=jax.ShapeDtypeStruct((LAGS * PARTS * GRO...  40.7 us
    unnamed x1, local copies, waits for them, and re-layouts  1.63 us

profile of v6, /device:TPU:1, one launch (start us, length us, event | category | flops | bytes accessed | tf_op | source)
XLA Modules:
  0.0 42.4 jit_solution(913432667531201223)
XLA Ops:
  0.0 40.7 %shard_map.91 = f32[408,128]{1,0:T(8,128)} custom-call(bf16[1500,256]{1,0:T(8,128)(2,1)} %bitcast.10, s32[1,256]{1,0:T(1,128)} %bitcast.11, bf16[512,1500]{1,0:T(8,128)(2,1)} %constant.14.clone.high_hbm, bf16[512,1500]{1,0:T(8,128)(2,1)} %constant.15.clone.rest_hbm, bf16[256,256]{1,0:T(8,128)(2,1)} %constant.16.clone.band_hbm, ...), custom_call_target="tpu_custom_call" | custom-call | tf_op jit(solution)/shard_map/pallas_call | solution.py:479
  40.7 1.6 %copy.12 = f32[4,51,256]{2,0,1:T(4,128)} copy(f32[4,51,256]{2,0,1:T(4,128)} %bitcast.9) | data formatting | bytes 417792

commit v7 on v6

--- a/solution.py
+++ b/solution.py
@@ -452,8 +452,13 @@
     own[1] = partial(1, 3, day)
     send_folded(0)
     send_folded(1)
-    terms = finish(0) + finish(1)
-    out[...] = jnp.dot(synth[...], jnp.concatenate(terms), preferred_element_type=F32)
+    depth = 3 * ROWS
+    out[...] = jnp.dot(
+        synth[:, 0:depth], jnp.concatenate(finish(0)), preferred_element_type=F32
+    )
+    out[...] += jnp.dot(
+        synth[:, depth:], jnp.concatenate(finish(1)), preferred_element_type=F32
+    )
 
     s_each("wait_send")
 

time: 42.5 us -> 42.4 us (level)
  no operation moved by 1% of the time
where the time goes in v7:
time: 42.4 us; the launch traced here: 42.3 us
  Pallas kernels  40.6 us (96%)
  local copies, waits for them, and re-layouts  1.63 us (4%)
    pallas_call x1, Pallas kernels, shards(): pl.pallas_call(kernel, out_shape=jax.ShapeDtypeStruct((LAGS * PARTS * GRO...  40.6 us
    unnamed x1, local copies, waits for them, and re-layouts  1.63 us

profile of v7, /device:TPU:1, one launch (start us, length us, event | category | flops | bytes accessed | tf_op | source)
XLA Modules:
  0.0 42.3 jit_solution(17208010898461665719)
XLA Ops:
  0.0 40.6 %shard_map.91 = f32[408,128]{1,0:T(8,128)} custom-call(bf16[1500,256]{1,0:T(8,128)(2,1)} %bitcast.10, s32[1,256]{1,0:T(1,128)} %bitcast.11, bf16[512,1500]{1,0:T(8,128)(2,1)} %constant.14.clone.high_hbm, bf16[512,1500]{1,0:T(8,128)(2,1)} %constant.15.clone.rest_hbm, bf16[256,256]{1,0:T(8,128)(2,1)} %constant.16.clone.band_hbm, ...), custom_call_target="tpu_custom_call" | custom-call | tf_op jit(solution)/shard_map/pallas_call | solution.py:484
  40.7 1.6 %copy.12 = f32[4,51,256]{2,0,1:T(4,128)} copy(f32[4,51,256]{2,0,1:T(4,128)} %bitcast.9) | data formatting | bytes 417792
